TPU v7x, 512 devices: a whole 4x4x16 slice. The times are simulated.
512 devices in a mesh: tok: 4 (over x_hi, core), qry: 8 (over x_lo, y), eig: 16 (over z).
Axes of the slice: x: 4 (x_hi: 2, x_lo: 2; x = x_hi * 2 + x_lo), y: 4, z: 16, core: 2. Of those that a mesh axis runs over, the one named last changes fastest.
Arguments:
- train_acts: bfloat16 [3072, 2560], P('tok', 'qry'), may hold values from -6 to 6
- train_grads: bfloat16 [3072, 6912], P('tok', 'qry'), may hold values from -6 to 6
- query_acts: bfloat16 [16, 32, 2560], P(None, None, 'qry'), may hold values from -6 to 6
- query_grads: bfloat16 [16, 32, 6912], P(None, None, 'qry'), may hold values from -6 to 6
- in_basis: bfloat16 [2560, 2560], P('qry', 'eig'), may hold values from -0.125 to 0.125
- out_basis: bfloat16 [6912, 6912], P('qry', 'eig'), may hold values from -0.078125 to 0.078125
- eigenvalues: float32 [6912, 2560], P('eig', 'tok'), may hold values from 0.01 to 324, as said below
Outputs:
- scores: float32 [3072, 16], P('tok', 'qry')
Inputs may be any that keep to these rules, and one draw needn't show every extreme that they name: `eigenvalues`: every entry is positive.
All inputs are finite; a program needn't handle non-finite values.
Results may differ from a plain program's by a relative error of at most 0.0048.
Values may be sent and summed in bfloat16 or wider, within the bound.
A program may use at most 64 MiB of HBM per device.

v0:
```python
import jax
import jax.numpy as jnp
from jax import lax
from jax.sharding import PartitionSpec as P

DIN = 2560
DOUT = 6912
LQ = 32


def shards(train_acts, train_grads, query_acts, query_grads, in_basis, out_basis, eigenvalues):
    grad_part = jnp.dot(train_grads, out_basis, preferred_element_type=jnp.float32)
    act_part = jnp.dot(train_acts, in_basis, preferred_element_type=jnp.float32)
    grad_sum, act_sum = lax.psum((grad_part, act_part), "qry")
    grad_proj = grad_sum.astype(jnp.bfloat16)
    act_local = act_sum.astype(jnp.bfloat16)
    queries, length = (query_grads.shape[0], query_grads.shape[1])
    qgrad_part = jnp.dot(
        query_grads.reshape(queries * length, query_grads.shape[2]),
        out_basis,
        preferred_element_type=jnp.float32,
    ).reshape(queries, length, out_basis.shape[1])
    qact_part = jnp.dot(
        query_acts.reshape(queries * length, query_acts.shape[2]),
        in_basis,
        preferred_element_type=jnp.float32,
    ).reshape(queries, length, in_basis.shape[1])
    out_sum, in_sum = (
        lax.psum_scatter(qgrad_part, "qry", scatter_dimension=0, tiled=True),
        lax.psum_scatter(qact_part, "qry", scatter_dimension=0, tiled=True),
    )
    query_out = out_sum.astype(jnp.bfloat16)
    query_in_local = in_sum.astype(jnp.bfloat16)
    act_proj, query_in = (
        lax.all_gather(act_local, "eig", axis=1, tiled=True),
        lax.all_gather(query_in_local, "eig", axis=2, tiled=True),
    )
    local_total = jnp.sum(eigenvalues)
    total = lax.psum(local_total, ("tok", "eig"))
    entries = (
        eigenvalues.shape[0] * eigenvalues.shape[1] * lax.axis_size("tok") * lax.axis_size("eig")
    )
    damping = 0.1 * (total / entries)
    outer = jnp.einsum("qld,qle->qde", query_out, query_in, preferred_element_type=jnp.float32)
    panel = (
        outer / (lax.all_gather(eigenvalues, "tok", axis=1, tiled=True) + damping)[None]
    ).astype(jnp.bfloat16)
    weighted = jnp.einsum("te,qde->qtd", act_proj, panel, preferred_element_type=jnp.float32)
    factor = 1.0 / jnp.sqrt(jnp.float32(LQ * DOUT * DIN))
    partial_scores = jnp.sum(weighted * grad_proj[None], axis=2) * factor
    summed = lax.psum(partial_scores, "eig")
    return summed.T


def solution(mesh):
    placed = (
        P("tok", "qry"),
        P("tok", "qry"),
        P(None, None, "qry"),
        P(None, None, "qry"),
        P("qry", "eig"),
        P("qry", "eig"),
        P("eig", "tok"),
    )
    return jax.shard_map(
        shards, mesh=mesh, in_specs=placed, out_specs=P("tok", "qry"), check_vma=False
    )
```

profile of v0, /device:TPU:4, one launch (start us, length us, event | category | flops | bytes accessed | tf_op | source)
XLA Modules:
  0.0 324.9 jit_solution(3211769699373787082)
XLA Ops:
  7.4 0.0 copy-start
  7.4 0.0 copy-start.4
  7.4 0.0 reduce-scatter.5.cloned.1.call-start
  7.4 2.3 fusion.11
  9.7 0.0 reduce-scatter.5.cloned.1.call-update
  9.7 0.0 copy-start.2
  9.7 0.0 copy-start.3
  9.7 0.0 all-gather.3.cloned.1.call-start
  9.8 0.5 all-gather.3.cloned.1.call-update
  10.3 0.0 reduce-scatter.3.cloned.1.call-start
  10.4 0.0 copy-done.4
  10.4 2.8 fusion.9
  13.2 0.0 reduce-scatter.3.cloned.1.call-update
  13.2 0.0 all-gather.5.cloned.1.call-start
  13.3 0.0 copy-done.2
  13.3 0.0 copy-done.3
  13.3 0.3 fusion.15
  13.6 0.0 copy-done
  13.6 3.1 fusion.16
  16.7 84.6 %all-reduce.2 = (bf16[768,432]{0,1:T(8,128)(2,1)}, bf16[768,160]{0,1:T(8,128)(2,1)}) all-reduce(f32[768,432]{0,1:T(8,128)} %fusion.16, f32[768,160]{0,1:T(8,128)S(1)} %fusion.15), channel_id=1, replica_groups=mesh['tok'=4,'qry'=8,'eig'=16] {'qry'}, use_global_device_ids=true, to_apply=%region_5.0 | all-reduce | flops 454656 | bytes 2727936 | tf_op jit(solution)/shard_map/psum | solution.py:14
  101.3 0.0 all-gather.5.cloned.1.call-update
  101.3 0.0 copy-done.1
  101.3 0.9 reduce_sum.18
  102.2 131.6 %psum.28 = f32[]{:T(128)} all-reduce(f32[]{:T(128)} %reduce_sum.18), channel_id=1, replica_groups=mesh['tok'=4,'qry'=8,'eig'=16] {'tok','eig'}, use_global_device_ids=true, to_apply=%region_3.0 | all-reduce | flops 1 | bytes 8 | tf_op jit(solution)/shard_map/psum | solution.py:39
  233.8 1.2 convert_element_type.35
  235.6 0.0 reduce-scatter.5.cloned.1.call-done
  235.7 0.8 convert_element_type.20
  236.5 0.1 copy.8
  236.6 37.0 %all_gather.9 = bf16[2,32,2560]{1,0,2:T(2,128)(2,1)} all-gather(bf16[2,32,160]{1,0,2:T(2,128)(2,1)S(1)} %copy.8), channel_id=1, replica_groups=mesh['tok'=4,'qry'=8,'eig'=16] {'eig'}, dimensions={2}, use_global_device_ids=true | all-gather | bytes 348160 | tf_op jit(solution)/shard_map/all_gather | solution.py:36
  273.6 4.6 %broadcast_add_fusion = f32[432,2560]{1,0:T(8,128)} fusion(f32[432,2560]{1,0:T(8,128)} %all-gather.3.cloned.1.call-done, f32[]{:T(128)S(6)} %mul_shard_map.3), kind=kLoop, calls=%fused_computation.5 | loop fusion | flops 1105920 | bytes 8847364 | tf_op jit(solution)/shard_map/add | solution.py:46
  278.2 8.7 %fusion.2 = f32[2,768]{1,0:T(2,128)S(1)} fusion(f32[768,432]{0,1:T(8,128)S(1)} %convert_element_type.35, bf16[768,2560]{0,1:T(8,128)(2,1)} %all-gather.5.cloned.1.call-done, f32[432,2560]{1,0:T(8,128)} %broadcast_add_fusion, bf16[2,32,2560]{1,0,2:T(2,128)(2,1)} %all_gather.9, f32[2,32,432]{2,1,0:T(8,128)} %reduce-scatter.3.cloned.1.call-done), kind=kOutput, calls=%fused_computation.4 | convolution fusion | flops 3544720896 | bytes 10127360 | tf_op jit(solution)/shard_map/te,qde->qtd/dot_general | solution.py:48
  287.0 30.5 %psum.31 = f32[768,2]{0,1:T(2,128)} all-reduce(f32[768,2]{0,1:T(2,128)S(1)} %multiply_bitcast_fusion), channel_id=1, replica_groups=mesh['tok'=4,'qry'=8,'eig'=16] {'eig'}, use_global_device_ids=true, to_apply=%region_7.0 | all-reduce | flops 1536 | bytes 12288 | tf_op jit(solution)/shard_map/psum | solution.py:51
  (5 shorter events, 0.0 us)
Async XLA Ops:
  7.4 6.2 %copy-start = (bf16[768,864]{0,1:T(8,128)(2,1)S(1)}, bf16[768,864]{0,1:T(8,128)(2,1)}, u32[]{:S(2)}) copy-start(bf16[768,864]{0,1:T(8,128)(2,1)} %param.8) | copy-start | bytes 3981316
  7.4 3.0 copy-start.4
  7.4 228.3 %reduce-scatter.5.cloned.1.call-start = ((), (), s32[]{:S(2)}) async-start(), calls=%async_computation.3 | async-start | bytes 589824 | tf_op jit(solution)/shard_map/reduce_scatter | solution.py:30
  9.7 3.6 %copy-start.2 = (bf16[768,320]{0,1:T(8,128)(2,1)S(1)}, bf16[768,320]{0,1:T(8,128)(2,1)}, u32[]{:S(2)}) copy-start(bf16[768,320]{0,1:T(8,128)(2,1)} %param.7) | copy-start | bytes 1474564
  9.7 3.6 %copy-start.3 = (bf16[320,160]{0,1:T(8,128)(2,1)S(1)}, bf16[320,160]{0,1:T(8,128)(2,1)}, u32[]{:S(2)}) copy-start(bf16[320,160]{0,1:T(8,128)(2,1)} %param.11) | copy-start | bytes 307204
  9.7 263.9 %all-gather.3.cloned.1.call-start = ((), (), s32[]{:S(2)}) async-start(), calls=%async_computation.4 | async-start | bytes 5529600 | tf_op jit(solution)/shard_map/all_gather | solution.py:46
  10.3 267.9 %reduce-scatter.3.cloned.1.call-start = ((), (), s32[]{:S(2)}) async-start(), calls=%async_computation.2 | async-start | bytes 1179648 | tf_op jit(solution)/shard_map/reduce_scatter | solution.py:29
  13.2 265.0 %all-gather.5.cloned.1.call-start = ((), (), s32[]{:S(2)}) async-start(), calls=%async_computation.5 | async-start | bytes 4177920 | tf_op jit(solution)/shard_map/all_gather | solution.py:35
  16.7 84.6 %copy-start.1 = (f32[432,640]{1,0:T(8,128)S(1)}, f32[432,640]{1,0:T(8,128)}, u32[]{:S(2)}) copy-start(f32[432,640]{1,0:T(8,128)} %param.13) | copy-start | bytes 3317764
Sparse Core Ops, SparseCore 0:
  11.0 86.8 reduce-scatter.4
  101.0 47.2 reduce-scatter.2
Sparse Core Ops, SparseCore 1:
  12.3 66.1 all-gather.2
  101.4 81.0 all-gather.4
where the time goes:
time: 325 us
  blocking collectives  284 us (87%)
  matrix products  17.2 us (5%)
  between operations  15.6 us (5%)
  other arithmetic  7.55 us (2%)
    psum x1, blocking collectives, shards(): total = lax.psum(local_total, ('tok', 'eig'))  132 us
    psum x1, blocking collectives, shards(): grad_sum, act_sum = lax.psum((grad_part, act_part), 'qry')  84.6 us
    all_gather x1, blocking collectives, shards(): lax.all_gather(query_in_local, 'eig', axis=2, tiled=True)  37 us
    psum x1, blocking collectives, shards(): summed = lax.psum(partial_scores, 'eig')  30.5 us
    dot_general x1, matrix products, shards(): jnp.einsum('te,qde->qtd', act_proj, panel, preferred_element_type=jnp.flo...  8.71 us
  transfers between devices with their start and end apart: 4, of which 0 were waited for; matrix products, arithmetic and copies ran while one was open for 4% of the time, Pallas kernels for 0%

commit v1 on v0

v1 whole, which is shorter than its diff:
```python
import functools

import jax
import jax.numpy as jnp
from jax import lax
from jax.experimental import pallas as pl
from jax.experimental.pallas import tpu as pltpu
from jax.sharding import PartitionSpec as P

DIN = 2560
DOUT = 6912
LQ = 32

MESH = pl.DeviceIdType.MESH
F32 = jnp.float32
BF16 = jnp.bfloat16

NT = 4
NF = 8
NZ = 16
ROWS = 768
SUB = 96
FI = 320
FO = 864
EI = 160
EO = 432
HALF = 1280
QROWS = 80
QP = 640
CHUNK = 256

NT_DIMS = (((1,), (1,)), ((), ()))


def dot(a, b):
    return jnp.dot(a, b, preferred_element_type=F32)


def rcopy(src, dst, send_sem, recv_sem, dev):
    return pltpu.make_async_remote_copy(
        src_ref=src,
        dst_ref=dst,
        send_sem=send_sem,
        recv_sem=recv_sem,
        device_id=dev,
        device_id_type=MESH,
    )


def kernel(
    ta_h, tg_h, qa_h, qg_h, v_h, u_h, ev_h,
    out_ref,
    ta, tg, qa, qg, v, u, ev,
    qpart, qrecv, qt, apart, arecv, at, gpart, grecv, gown, gt_own, gt,
    evb, evh, rinv, za, zq, pan, tsum, trecv, zsum, zrecv,
    stage, srecv, fsum, frecv,
    in_sem,
    q_s, q_r, qg_s, qg_r, a_s, a_r, g_s, g_r,
    sib_s, sib_r, ga_s, ga_r, ev_s, ev_r, t_s, t_r, zs_s, zs_r,
    rq_s, rq_r, ra_s, ra_r, pa_s, pa_r, sc_s, sc_r, fz_s, fz_r,
):
    tok = lax.axis_index("tok")
    qry = lax.axis_index("qry")
    z = lax.axis_index("eig")
    c = tok % 2
    xh = tok // 2
    xl = qry // 4
    y = qry % 4
    sib = (xh * 2 + 1 - c, qry, z)
    pqry = (1 - xl) * 4 + y
    slot = z % 8
    owner = z // 8 == c

    loads = []
    for n, (src, dst) in enumerate(
        (
            (qg_h.at[pl.ds(tok * 128, 128)], qg),
            (u_h, u),
            (qa_h.at[pl.ds(tok * 128, 128)], qa),
            (v_h, v),
            (ta_h, ta),
            (ev_h, ev),
            (tg_h, tg),
        )
    ):
        load = pltpu.make_async_copy(src, dst, in_sem.at[n])
        load.start()
        loads.append(load)

    barrier = pltpu.get_barrier_semaphore()
    for dt in range(NT):
        for df in range(NF):
            if dt or df:
                pl.semaphore_signal(
                    barrier,
                    inc=1,
                    device_id=((tok + dt) % NT, (qry + df) % NF, z),
                    device_id_type=MESH,
                )
    for dz in range(1, NZ):
        pl.semaphore_signal(
            barrier, inc=1, device_id=(tok, qry, (z + dz) % NZ), device_id_type=MESH
        )

    for n in range(4):
        loads[n].wait()
    qpart[0:EO, :] = dot(qg[...], u[...]).T
    qpart[EO : EO + EI, :] = dot(qa[...], v[...]).T
    qpart[EO + EI :, :] = jnp.zeros((QP - EO - EI, 128), F32)

    pl.semaphore_wait(barrier, NT * NF - 1 + NZ - 1)

    def q_copy(k):
        to = (qry + k) % NF
        return rcopy(
            qpart.at[pl.ds(pl.multiple_of(to * QROWS, 16), QROWS)],
            qrecv.at[k],
            q_s.at[k],
            q_r.at[k],
            (tok, to, z),
        )

    for k in range(1, NF):
        q_copy(k).start()

    loads[4].wait()
    apart[...] = dot(ta[...], v[...]).astype(BF16)

    def a_copy(k):
        to = (qry + k) % NF
        return rcopy(
            apart.at[pl.ds(pl.multiple_of(to * SUB, 16), SUB)],
            arecv.at[k],
            a_s.at[k],
            a_r.at[k],
            (tok, to, z),
        )

    for k in range(1, NF):
        a_copy(k).start()

    loads[5].wait()
    evals = ev[...]
    evb[...] = evals.astype(BF16)
    rows8 = jnp.sum(evals.reshape(EO // 8, 8, 640), axis=0)
    tsum[...] = sum(rows8[:, 128 * n : 128 * n + 128] for n in range(5))

    def t_copy(dt):
        return rcopy(
            tsum, trecv.at[dt], t_s.at[dt], t_r.at[dt], ((tok + dt) % NT, qry, z)
        )

    for dt in range(1, NT):
        t_copy(dt).start()

    def ev_far():
        return rcopy(
            evb, evh.at[c], ev_s.at[0], ev_r.at[c], ((1 - xh) * 2 + xh, pqry, z)
        )

    def ev_near():
        return rcopy(evb, evh.at[c], ev_s.at[1], ev_r.at[c], sib)

    ev_far().start()

    @pl.when(c == xh)
    def _():
        evh[c] = evb[...]

    @pl.when(c != xh)
    def _():
        ev_near().start()

    for k in range(1, NF):
        q_copy(k).wait_recv()
    mine = qpart[pl.ds(pl.multiple_of(qry * QROWS, 16), QROWS), :]
    for k in range(1, NF):
        mine = mine + qrecv[k]
    qt[c, pl.ds(pl.multiple_of(qry * QROWS, 16), QROWS), :] = mine.astype(BF16)

    def qg_copy(dc, k):
        block = qt.at[c, pl.ds(pl.multiple_of(qry * QROWS, 16), QROWS)]
        return rcopy(
            block,
            block,
            qg_s.at[dc, k],
            qg_r.at[dc, k],
            (xh * 2 + (c + dc) % 2, (qry + k) % NF, z),
        )

    def qg_arrival(dc, k):
        frm = (qry - k + NF) % NF
        block = qt.at[
            (c + dc) % 2, pl.ds(pl.multiple_of(frm * QROWS, 16), QROWS)
        ]
        return rcopy(block, block, qg_s.at[dc, k], qg_r.at[dc, k], sib)

    peers = [(dc, k) for k in range(NF) for dc in range(2) if dc or k]
    for dc, k in peers:
        qg_copy(dc, k).start()

    for k in range(1, NF):
        a_copy(k).wait_recv()
    asum = apart[pl.ds(pl.multiple_of(qry * SUB, 16), SUB), :].astype(F32)
    for k in range(1, NF):
        asum = asum + arecv[k].astype(F32)
    asum = jnp.concatenate([asum, jnp.zeros((128 - SUB, EI), F32)], axis=0)
    at[...] = asum.T.astype(BF16)

    my_rows = pl.ds(pl.multiple_of(slot * EI, 16), EI)
    my_lanes = pl.ds(pl.multiple_of(c * 128, 128), 128)
    sib_lanes = pl.ds(pl.multiple_of((1 - c) * 128, 128), 128)

    def sib_copy():
        return rcopy(at, za.at[my_rows, my_lanes], sib_s.at[0], sib_r.at[0], sib)

    @pl.when(owner)
    def _():
        za[my_rows, my_lanes] = at[...]

    @pl.when(jnp.logical_not(owner))
    def _():
        sib_copy().start()

    for dt in range(1, NT):
        t_copy(dt).wait_recv()
    zsum[...] = tsum[...] + trecv[1] + trecv[2] + trecv[3]

    def zs_copy(dz):
        return rcopy(
            zsum, zrecv.at[dz], zs_s.at[dz], zs_r.at[dz], (tok, qry, (z + dz) % NZ)
        )

    for dz in range(1, NZ):
        zs_copy(dz).start()

    up = (tok, qry, (z + 1) % NZ)
    down = (tok, qry, (z + NZ - 1) % NZ)

    def blk(buf, s):
        rows = pl.ds(pl.multiple_of(s * EI, 16), EI)
        return buf.at[rows, pl.ds(0, 256)]

    def hop(buf, sends, recvs, s, way):
        return rcopy(
            blk(buf, s), blk(buf, s), sends.at[way, s], recvs.at[s], (up, down)[way]
        )

    def ring_open(buf, sends, recvs):
        hop(buf, sends, recvs, slot, 0).start()
        hop(buf, sends, recvs, slot, 1).start()

    def ring_step(buf, sends, recvs, s, after=None):
        for way, last in ((0, 8), (1, 7)):
            if s > last:
                continue
            origin = (z + NZ - s) % NZ if way == 0 else (z + s) % NZ

            @pl.when(origin // 8 == c)
            def _():
                hop(buf, sends, recvs, origin % 8, way).wait_recv()
                if s < last:
                    hop(buf, sends, recvs, origin % 8, way).start()
                if after is not None:
                    after(origin % 8)

    def ring_close(buf, sends, recvs):
        for s in range(8):
            for way, last in ((0, 8), (1, 7)):
                if s >= last:
                    continue
                origin = (z + NZ - s) % NZ if way == 0 else (z + s) % NZ

                @pl.when(origin // 8 == c)
                def _():
                    hop(buf, sends, recvs, origin % 8, way).wait_send()

    def pa_copy(s):
        rows = pl.ds(pl.multiple_of(s * EI, 16), EI)
        return rcopy(
            za.at[rows, pl.ds(0, 256)],
            za.at[rows, pl.ds(256, 256)],
            pa_s.at[s],
            pa_r.at[s],
            ((1 - xh) * 2 + c, pqry, z),
        )

    for dc, k in peers:
        qg_arrival(dc, k).wait_recv()

    @pl.when(owner)
    def _():
        for n in range(2):
            zq[my_rows, 128 * n : 128 * n + 128] = qt[n, EO : EO + EI, :]
        ring_open(zq, rq_s, rq_r)
        rcopy(
            at, za.at[my_rows, sib_lanes], sib_s.at[0], sib_r.at[0], sib
        ).wait_recv()
        ring_open(za, ra_s, ra_r)
        pa_copy(slot).start()

    loads[6].wait()

    def g_copy(k):
        return rcopy(
            gpart.at[k], grecv.at[k], g_s.at[k], g_r.at[k], (tok, (qry + k) % NF, z)
        )

    for k in range(1, NF + 1):
        to = (qry + k) % NF
        rows = pl.ds(pl.multiple_of(to * SUB, 16), SUB)
        part = dot(tg[rows, :], u[...])
        if k < NF:
            gpart[k] = part.astype(BF16)
            g_copy(k).start()
        else:
            gown[...] = part
        ring_step(zq, rq_s, rq_r, k)

    for dz in range(1, NZ):
        zs_copy(dz).wait_recv()
    total = zsum[...]
    for dz in range(1, NZ):
        total = total + zrecv[dz]
    damping = 0.1 * (jnp.sum(total) / (DIN * DOUT))

    ev_other = rcopy(evb, evh.at[1 - c], ev_s.at[0], ev_r.at[1 - c], sib)
    ev_other.wait_recv()

    @pl.when(c != xh)
    def _():
        rcopy(evb, evh.at[c], ev_s.at[0], ev_r.at[c], sib).wait_recv()

    for n in range(2):
        rinv[:, 640 * n : 640 * n + 640] = 1.0 / (evh[n].astype(F32) + damping)

    qot = jnp.concatenate([qt[0, 0:EO, :], qt[1, 0:EO, :]], axis=1)
    lane = lax.broadcasted_iota(jnp.int32, (EO, 256), 1) // LQ

    def panel(q, carry):
        left = jnp.where(lane == q, qot, jnp.zeros_like(qot))
        for n in range(HALF // CHUNK):
            cols = slice(CHUNK * n, CHUNK * n + CHUNK)
            outer = lax.dot_general(
                left, zq[cols, :], NT_DIMS, preferred_element_type=F32
            )
            pan[q, :, cols] = (outer * rinv[:, cols]).astype(BF16)
        return carry

    for s in range(1, 9):
        ring_step(za, ra_s, ra_r, s, lambda o: pa_copy(o).start())
        panel(s - 1, 0)

    for k in range(1, NF):
        g_copy(k).wait_recv()
    gsum = gown[...]
    for k in range(1, NF):
        gsum = gsum + grecv[k].astype(F32)
    gsum = jnp.concatenate([gsum, jnp.zeros((128 - SUB, EO), F32)], axis=0)
    gt_own[...] = gsum.T.astype(BF16)
    gt[:, my_lanes] = gt_own[...]
    far_lanes = pl.ds(pl.multiple_of(256 + c * 128, 128), 128)

    ga_copies = [
        rcopy(gt_own, gt.at[:, my_lanes], ga_s.at[0], ga_r.at[0], sib),
        rcopy(
            gt_own, gt.at[:, far_lanes], ga_s.at[1], ga_r.at[1 + c],
            ((1 - xh) * 2, pqry, z),
        ),
        rcopy(
            gt_own, gt.at[:, far_lanes], ga_s.at[2], ga_r.at[1 + c],
            ((1 - xh) * 2 + 1, pqry, z),
        ),
    ]
    for copy in ga_copies:
        copy.start()

    for s in range(8):
        pa_arrival = rcopy(
            za.at[pl.ds(s * EI, EI), pl.ds(0, 256)],
            za.at[pl.ds(s * EI, EI), pl.ds(256, 256)],
            pa_s.at[s],
            pa_r.at[s],
            sib,
        )
        pa_arrival.wait_recv()
    rcopy(gt_own, gt.at[:, sib_lanes], ga_s.at[0], ga_r.at[0], sib).wait_recv()
    for n in range(2):
        lanes = pl.ds(256 + 128 * n, 128)
        rcopy(gt_own, gt.at[:, lanes], ga_s.at[1], ga_r.at[1 + n], sib).wait_recv()

    for q in range(8):
        weighted = dot(pan[q], za[...])
        row = jnp.sum(weighted * gt[...].astype(F32), axis=0, keepdims=True)
        for g in range(4):
            stage[q // 2, g, q % 2 : q % 2 + 1, :] = row[:, 128 * g : 128 * g + 128]

    def sc_copy(k, g):
        if g < 2:
            to_tok, frm = xh * 2 + g, qry
        else:
            to_tok, frm = (1 - xh) * 2 + g - 2, pqry
        return (
            rcopy(
                stage.at[k, g],
                srecv.at[c, frm],
                sc_s.at[k, g],
                sc_r.at[c, frm],
                (to_tok, xh * 4 + k, z),
            ),
            (to_tok == tok) & (xh * 4 + k == qry),
        )

    for k in range(4):
        for g in range(4):
            copy, here = sc_copy(k, g)
            if g < 2:

                @pl.when(here)
                def _():
                    srecv[c, qry] = stage[k, g]

                @pl.when(jnp.logical_not(here))
                def _():
                    copy.start()

            else:
                copy.start()

    for n in range(2):
        for f in range(NF):

            @pl.when(jnp.logical_not((c == n) & (qry == f) & (xh == xl)))
            def _():
                rcopy(
                    stage.at[0, 0], srecv.at[n, f], sc_s.at[0, 0], sc_r.at[n, f], sib
                ).wait_recv()

    factor = 1.0 / jnp.sqrt(F32(LQ * DOUT * DIN))
    for f in range(NF):
        fsum[2 * f : 2 * f + 2, :] = (srecv[0, f, 0:2, :] + srecv[1, f, 0:2, :]) * factor

    def fz_copy(dz):
        return rcopy(
            fsum, frecv.at[dz], fz_s.at[dz], fz_r.at[dz], (tok, qry, (z + dz) % NZ)
        )

    for dz in range(1, NZ):
        fz_copy(dz).start()
    for dz in range(1, NZ):
        fz_copy(dz).wait_recv()
    scores = fsum[...]
    for dz in range(1, NZ):
        scores = scores + frecv[dz]
    out_ref[...] = scores

    for k in range(1, NF):
        q_copy(k).wait_send()
        a_copy(k).wait_send()
        g_copy(k).wait_send()
    for dt in range(1, NT):
        t_copy(dt).wait_send()
    ev_far().wait_send()

    @pl.when(c != xh)
    def _():
        ev_near().wait_send()

    for dc, k in peers:
        qg_copy(dc, k).wait_send()

    @pl.when(jnp.logical_not(owner))
    def _():
        sib_copy().wait_send()

    for dz in range(1, NZ):
        zs_copy(dz).wait_send()
        fz_copy(dz).wait_send()
    ring_close(zq, rq_s, rq_r)
    ring_close(za, ra_s, ra_r)
    for s in range(8):
        pa_copy(s).wait_send()
    for copy in ga_copies:
        copy.wait_send()
    for k in range(4):
        for g in range(4):
            copy, here = sc_copy(k, g)
            if g < 2:

                @pl.when(jnp.logical_not(here))
                def _():
                    copy.wait_send()

            else:
                copy.wait_send()


def shards(train_acts, train_grads, query_acts, query_grads, in_basis, out_basis, eigenvalues):
    dma = pltpu.SemaphoreType.DMA
    vm = pltpu.VMEM
    out = pl.pallas_call(
        kernel,
        out_shape=jax.ShapeDtypeStruct((16, 128), F32),
        in_specs=[pl.BlockSpec(memory_space=pl.ANY)] * 7,
        out_specs=pl.BlockSpec(memory_space=pltpu.VMEM),
        scratch_shapes=[
            vm((ROWS, FI), BF16), vm((ROWS, FO), BF16), vm((128, FI), BF16),
            vm((128, FO), BF16), vm((FI, EI), BF16), vm((FO, EO), BF16),
            vm((EO, 640), F32),
            vm((QP, 128), F32), vm((NF, QROWS, 128), F32), vm((2, QP, 128), BF16),
            vm((ROWS, EI), BF16), vm((NF, SUB, EI), BF16), vm((EI, 128), BF16),
            vm((NF, SUB, EO), BF16), vm((NF, SUB, EO), BF16), vm((SUB, EO), F32),
            vm((EO, 128), BF16), vm((EO, 512), BF16),
            vm((EO, 640), BF16), vm((2, EO, 640), BF16), vm((EO, HALF), F32),
            vm((HALF, 512), BF16), vm((HALF, 256), BF16), vm((8, EO, HALF), BF16),
            vm((8, 128), F32), vm((NT, 8, 128), F32),
            vm((8, 128), F32), vm((NZ, 8, 128), F32),
            vm((4, 4, 8, 128), F32), vm((2, NF, 8, 128), F32),
            vm((16, 128), F32), vm((NZ, 16, 128), F32),
            dma((7,)),
            dma((NF,)), dma((NF,)), dma((2, NF)), dma((2, NF)),
            dma((NF,)), dma((NF,)), dma((NF,)), dma((NF,)),
            dma((1,)), dma((1,)), dma((3,)), dma((3,)),
            dma((2,)), dma((2,)), dma((NT,)), dma((NT,)), dma((NZ,)), dma((NZ,)),
            dma((2, 8)), dma((8,)), dma((2, 8)), dma((8,)),
            dma((8,)), dma((8,)), dma((4, 4)), dma((2, NF)), dma((NZ,)), dma((NZ,)),
        ],
        compiler_params=pltpu.CompilerParams(
            collective_id=0, has_side_effects=True, vmem_limit_bytes=56 * 1024 * 1024
        ),
    )(
        train_acts,
        train_grads,
        query_acts.reshape(16 * LQ, FI),
        query_grads.reshape(16 * LQ, FO),
        in_basis,
        out_basis,
        eigenvalues,
    )
    return out.reshape(NF, 2, 128)[:, :, :SUB].transpose(0, 2, 1).reshape(ROWS, 2)


def solution(mesh):
    placed = (
        P("tok", "qry"),
        P("tok", "qry"),
        P(None, None, "qry"),
        P(None, None, "qry"),
        P("qry", "eig"),
        P("qry", "eig"),
        P("eig", "tok"),
    )
    return jax.shard_map(
        shards, mesh=mesh, in_specs=placed, out_specs=P("tok", "qry"), check_vma=False
    )
```

time: 325 us -> 120 us (0.37)
  the two profiles are of different devices: /device:TPU:4 before, /device:TPU:1 now
where the time goes in v1:
time: 120 us
  Pallas kernels  112 us (93%)
  local copies, waits for them, and re-layouts  8.38 us (7%)
    pallas_call x1, Pallas kernels, shards(): pl.pallas_call(kernel, out_shape=jax.ShapeDtypeStruct((16, 128), F32), in...  112 us
    unnamed x8, local copies, waits for them, and re-layouts  7 us

profile of v1, /device:TPU:1, one launch (start us, length us, event | category | flops | bytes accessed | tf_op | source)
XLA Modules:
  0.0 119.9 jit_solution(12937145792168377488)
XLA Ops:
  0.0 0.0 copy-start.1
  0.0 1.8 %copy.10.v_h = bf16[320,160]{1,0:T(8,128)(2,1)} copy(bf16[320,160]{0,1:T(8,128)(2,1)} %param.11) | data formatting | bytes 204800 | tf_op args[4]
  1.8 0.0 copy-start
  1.8 2.2 %copy.8.ta_h = bf16[768,320]{1,0:T(8,128)(2,1)} copy(bf16[768,320]{0,1:T(8,128)(2,1)} %param.7) | data formatting | bytes 983040 | tf_op args[0]
  4.0 0.0 copy-done.1
  4.0 1.5 %copy.11.u_h = bf16[864,432]{1,0:T(8,128)(2,1)} copy(bf16[864,432]{0,1:T(8,128)(2,1)S(1)} %copy-done.1) | data formatting | bytes 1492992 | tf_op args[5]
  5.4 0.0 copy-done
  5.5 1.6 %copy.9.tg_h = bf16[768,864]{1,0:T(8,128)(2,1)} copy(bf16[768,864]{0,1:T(8,128)(2,1)S(1)} %copy-done) | data formatting | bytes 2654208 | tf_op args[1]
  7.0 111.5 %shard_map.73 = f32[16,128]{1,0:T(8,128)} custom-call(bf16[768,320]{1,0:T(8,128)(2,1)} %copy.8.ta_h, bf16[768,864]{1,0:T(8,128)(2,1)} %copy.9.tg_h, bf16[512,320]{1,0:T(8,128)(2,1)} %bitcast.8, bf16[512,864]{1,0:T(8,128)(2,1)} %bitcast.7, bf16[320,160]{1,0:T(8,128)(2,1)} %copy.10.v_h, bf16[864,432]{1,0:T(8,128)(2,1)} %copy.11.u_h, f32[432,640]{1,0:T(8,128)} %ev_h.1), custom_call_target="tpu_custom_call" | custom-call | tf_op jit(solution)/shard_map/pallas_call | solution.py:501
  118.6 0.7 slice_bitcast_fusion
  119.3 0.7 reshape.15
  (1 shorter events, 0.0 us)
Async XLA Ops:
  0.0 4.0 %copy-start.1 = (bf16[864,432]{0,1:T(8,128)(2,1)S(1)}, bf16[864,432]{0,1:T(8,128)(2,1)}, u32[]{:S(2)}) copy-start(bf16[864,432]{0,1:T(8,128)(2,1)} %param.12) | copy-start | bytes 2239492
  1.8 3.7 %copy-start = (bf16[768,864]{0,1:T(8,128)(2,1)S(1)}, bf16[768,864]{0,1:T(8,128)(2,1)}, u32[]{:S(2)}) copy-start(bf16[768,864]{0,1:T(8,128)(2,1)} %param.8) | copy-start | bytes 3981316

commit v2 on v1

--- a/solution.py
+++ b/solution.py
@@ -29,11 +29,25 @@
 QP = 640
 CHUNK = 256
 
+TREE = {0: (3, -3, 1, -1), 3: (3, 1, -1), -3: (-3, -1, 1), 6: (2, 1, -1), -6: (-1, 1)}
+NEAR = (1, -1, 2, -2, 3, -3)
+
 NT_DIMS = (((1,), (1,)), ((), ()))
 
 
 def dot(a, b):
     return jnp.dot(a, b, preferred_element_type=F32)
+
+
+def dot_nt(a, b):
+    return lax.dot_general(a, b, NT_DIMS, preferred_element_type=F32)
+
+
+def lanes_of(whole, f):
+    part = whole[:, SUB * f : SUB * f + SUB]
+    return jnp.concatenate(
+        [part, jnp.zeros((part.shape[0], 128 - SUB), part.dtype)], axis=1
+    )
 
 
 def rcopy(src, dst, send_sem, recv_sem, dev):
@@ -51,7 +65,7 @@
     ta_h, tg_h, qa_h, qg_h, v_h, u_h, ev_h,
     out_ref,
     ta, tg, qa, qg, v, u, ev,
-    qpart, qrecv, qt, apart, arecv, at, gpart, grecv, gown, gt_own, gt,
+    qpart, qrecv, qt, apart, arecv, at, gpart, grecv, gt_own, gt,
     evb, evh, rinv, za, zq, pan, tsum, trecv, zsum, zrecv,
     stage, srecv, fsum, frecv,
     in_sem,
@@ -97,18 +111,21 @@
                     device_id=((tok + dt) % NT, (qry + df) % NF, z),
                     device_id_type=MESH,
                 )
-    for dz in range(1, NZ):
+    for dz in NEAR:
         pl.semaphore_signal(
-            barrier, inc=1, device_id=(tok, qry, (z + dz) % NZ), device_id_type=MESH
+            barrier,
+            inc=1,
+            device_id=(tok, qry, (z + dz + NZ) % NZ),
+            device_id_type=MESH,
         )
 
     for n in range(4):
         loads[n].wait()
-    qpart[0:EO, :] = dot(qg[...], u[...]).T
-    qpart[EO : EO + EI, :] = dot(qa[...], v[...]).T
+    qpart[0:EO, :] = dot_nt(u[...], qg[...])
+    qpart[EO : EO + EI, :] = dot_nt(v[...], qa[...])
     qpart[EO + EI :, :] = jnp.zeros((QP - EO - EI, 128), F32)
 
-    pl.semaphore_wait(barrier, NT * NF - 1 + NZ - 1)
+    pl.semaphore_wait(barrier, NT * NF - 1 + len(NEAR))
 
     def q_copy(k):
         to = (qry + k) % NF
@@ -124,17 +141,13 @@
         q_copy(k).start()
 
     loads[4].wait()
-    apart[...] = dot(ta[...], v[...]).astype(BF16)
+    a_all = dot(v[...], ta[...]).astype(BF16)
+    for f in range(NF):
+        apart[f] = lanes_of(a_all, f)
 
     def a_copy(k):
         to = (qry + k) % NF
-        return rcopy(
-            apart.at[pl.ds(pl.multiple_of(to * SUB, 16), SUB)],
-            arecv.at[k],
-            a_s.at[k],
-            a_r.at[k],
-            (tok, to, z),
-        )
+        return rcopy(apart.at[to], arecv.at[k], a_s.at[k], a_r.at[k], (tok, to, z))
 
     for k in range(1, NF):
         a_copy(k).start()
@@ -170,6 +183,13 @@
     @pl.when(c != xh)
     def _():
         ev_near().start()
+
+    loads[6].wait()
+    for half in range(2):
+        lanes = slice(384 * half, 384 * half + 384)
+        g_all = dot(u[...], tg[:, lanes]).astype(BF16)
+        for f in range(4):
+            gpart[4 * half + f] = lanes_of(g_all, f)
 
     for k in range(1, NF):
         q_copy(k).wait_recv()
@@ -201,11 +221,17 @@
 
     for k in range(1, NF):
         a_copy(k).wait_recv()
-    asum = apart[pl.ds(pl.multiple_of(qry * SUB, 16), SUB), :].astype(F32)
+    asum = apart[qry].astype(F32)
     for k in range(1, NF):
         asum = asum + arecv[k].astype(F32)
-    asum = jnp.concatenate([asum, jnp.zeros((128 - SUB, EI), F32)], axis=0)
-    at[...] = asum.T.astype(BF16)
+    for dt in range(1, NT):
+        t_copy(dt).wait_recv()
+    plane_sum = jnp.sum(tsum[...] + trecv[1] + trecv[2] + trecv[3], keepdims=True)
+    high = plane_sum.astype(BF16).astype(F32)
+    spot = lax.broadcasted_iota(jnp.int32, (EI, 128), 1)
+    asum = jnp.where(spot == SUB, high, asum)
+    asum = jnp.where(spot == SUB + 1, plane_sum - high, asum)
+    at[...] = asum.astype(BF16)
 
     my_rows = pl.ds(pl.multiple_of(slot * EI, 16), EI)
     my_lanes = pl.ds(pl.multiple_of(c * 128, 128), 128)
@@ -222,58 +248,42 @@
     def _():
         sib_copy().start()
 
-    for dt in range(1, NT):
-        t_copy(dt).wait_recv()
-    zsum[...] = tsum[...] + trecv[1] + trecv[2] + trecv[3]
-
-    def zs_copy(dz):
-        return rcopy(
-            zsum, zrecv.at[dz], zs_s.at[dz], zs_r.at[dz], (tok, qry, (z + dz) % NZ)
-        )
-
-    for dz in range(1, NZ):
-        zs_copy(dz).start()
-
-    up = (tok, qry, (z + 1) % NZ)
-    down = (tok, qry, (z + NZ - 1) % NZ)
-
     def blk(buf, s):
         rows = pl.ds(pl.multiple_of(s * EI, 16), EI)
         return buf.at[rows, pl.ds(0, 256)]
 
-    def hop(buf, sends, recvs, s, way):
-        return rcopy(
-            blk(buf, s), blk(buf, s), sends.at[way, s], recvs.at[s], (up, down)[way]
-        )
-
-    def ring_open(buf, sends, recvs):
-        hop(buf, sends, recvs, slot, 0).start()
-        hop(buf, sends, recvs, slot, 1).start()
-
-    def ring_step(buf, sends, recvs, s, after=None):
-        for way, last in ((0, 8), (1, 7)):
-            if s > last:
-                continue
-            origin = (z + NZ - s) % NZ if way == 0 else (z + s) % NZ
+    def hop(buf, sends, recvs, s, n, by):
+        return rcopy(
+            blk(buf, s),
+            blk(buf, s),
+            sends.at[n, s],
+            recvs.at[s],
+            (tok, qry, (z + by + NZ) % NZ),
+        )
+
+    def gather_open(buf, sends, recvs):
+        for n, by in enumerate(TREE[0]):
+            hop(buf, sends, recvs, slot, n, by).start()
+
+    def gather_step(buf, sends, recvs, far, after=None):
+        origin = (z - far + NZ) % NZ
+
+        @pl.when(origin // 8 == c)
+        def _():
+            hop(buf, sends, recvs, origin % 8, 0, 1).wait_recv()
+            for n, by in enumerate(TREE.get(far, ())):
+                hop(buf, sends, recvs, origin % 8, n, by).start()
+            if after is not None:
+                after(origin % 8)
+
+    def gather_close(buf, sends, recvs):
+        for far, on in TREE.items():
+            origin = (z - far + NZ) % NZ
 
             @pl.when(origin // 8 == c)
             def _():
-                hop(buf, sends, recvs, origin % 8, way).wait_recv()
-                if s < last:
-                    hop(buf, sends, recvs, origin % 8, way).start()
-                if after is not None:
-                    after(origin % 8)
-
-    def ring_close(buf, sends, recvs):
-        for s in range(8):
-            for way, last in ((0, 8), (1, 7)):
-                if s >= last:
-                    continue
-                origin = (z + NZ - s) % NZ if way == 0 else (z + s) % NZ
-
-                @pl.when(origin // 8 == c)
-                def _():
-                    hop(buf, sends, recvs, origin % 8, way).wait_send()
+                for n, by in enumerate(on):
+                    hop(buf, sends, recvs, origin % 8, n, by).wait_send()
 
     def pa_copy(s):
         rows = pl.ds(pl.multiple_of(s * EI, 16), EI)
@@ -285,44 +295,51 @@
             ((1 - xh) * 2 + c, pqry, z),
         )
 
-    for dc, k in peers:
-        qg_arrival(dc, k).wait_recv()
-
     @pl.when(owner)
     def _():
-        for n in range(2):
-            zq[my_rows, 128 * n : 128 * n + 128] = qt[n, EO : EO + EI, :]
-        ring_open(zq, rq_s, rq_r)
         rcopy(
             at, za.at[my_rows, sib_lanes], sib_s.at[0], sib_r.at[0], sib
         ).wait_recv()
-        ring_open(za, ra_s, ra_r)
+        gather_open(za, ra_s, ra_r)
         pa_copy(slot).start()
 
-    loads[6].wait()
+    for dc, k in peers:
+        qg_arrival(dc, k).wait_recv()
+
+    @pl.when(owner)
+    def _():
+        for n in range(2):
+            zq[my_rows, 128 * n : 128 * n + 128] = qt[n, EO : EO + EI, :]
+        gather_open(zq, rq_s, rq_r)
 
     def g_copy(k):
         return rcopy(
-            gpart.at[k], grecv.at[k], g_s.at[k], g_r.at[k], (tok, (qry + k) % NF, z)
-        )
-
-    for k in range(1, NF + 1):
-        to = (qry + k) % NF
-        rows = pl.ds(pl.multiple_of(to * SUB, 16), SUB)
-        part = dot(tg[rows, :], u[...])
-        if k < NF:
-            gpart[k] = part.astype(BF16)
-            g_copy(k).start()
-        else:
-            gown[...] = part
-        ring_step(zq, rq_s, rq_r, k)
-
-    for dz in range(1, NZ):
-        zs_copy(dz).wait_recv()
-    total = zsum[...]
-    for dz in range(1, NZ):
-        total = total + zrecv[dz]
-    damping = 0.1 * (jnp.sum(total) / (DIN * DOUT))
+            gpart.at[(qry + k) % NF],
+            grecv.at[k],
+            g_s.at[k],
+            g_r.at[k],
+            (tok, (qry + k) % NF, z),
+        )
+
+    for k in range(1, NF):
+        g_copy(k).start()
+
+    for far in (3, -3, 6, -6):
+        gather_step(za, ra_s, ra_r, far, lambda o: pa_copy(o).start())
+        gather_step(zq, rq_s, rq_r, far)
+    for far in (1, -1, 2, -2, 4, -4, 5, -5, 7, -7, 8):
+        gather_step(za, ra_s, ra_r, far, lambda o: pa_copy(o).start())
+        gather_step(zq, rq_s, rq_r, far)
+
+    half_sum = jnp.zeros((1, 2), F32)
+    for n in range(8):
+        half_sum = half_sum + za[EI * n : EI * n + 16, SUB : SUB + 2].astype(F32)[0:1]
+    half_sum = jnp.sum(half_sum, keepdims=True)
+    zsum[...] = jnp.broadcast_to(half_sum, (8, 128))
+    zs_copy = rcopy(zsum, zrecv, zs_s.at[0], zs_r.at[0], sib)
+    zs_copy.start()
+    zs_copy.wait_recv()
+    damping = 0.1 * ((zsum[0:1, 0:1] + zrecv[0:1, 0:1]) / (DIN * DOUT))
 
     ev_other = rcopy(evb, evh.at[1 - c], ev_s.at[0], ev_r.at[1 - c], sib)
     ev_other.wait_recv()
@@ -337,27 +354,22 @@
     qot = jnp.concatenate([qt[0, 0:EO, :], qt[1, 0:EO, :]], axis=1)
     lane = lax.broadcasted_iota(jnp.int32, (EO, 256), 1) // LQ
 
-    def panel(q, carry):
+    def panel(q):
         left = jnp.where(lane == q, qot, jnp.zeros_like(qot))
         for n in range(HALF // CHUNK):
             cols = slice(CHUNK * n, CHUNK * n + CHUNK)
-            outer = lax.dot_general(
-                left, zq[cols, :], NT_DIMS, preferred_element_type=F32
-            )
+            outer = dot_nt(left, zq[cols, :])
             pan[q, :, cols] = (outer * rinv[:, cols]).astype(BF16)
-        return carry
-
-    for s in range(1, 9):
-        ring_step(za, ra_s, ra_r, s, lambda o: pa_copy(o).start())
-        panel(s - 1, 0)
+
+    for q in range(8):
+        panel(q)
 
     for k in range(1, NF):
         g_copy(k).wait_recv()
-    gsum = gown[...]
+    gsum = gpart[qry].astype(F32)
     for k in range(1, NF):
         gsum = gsum + grecv[k].astype(F32)
-    gsum = jnp.concatenate([gsum, jnp.zeros((128 - SUB, EO), F32)], axis=0)
-    gt_own[...] = gsum.T.astype(BF16)
+    gt_own[...] = gsum.astype(BF16)
     gt[:, my_lanes] = gt_own[...]
     far_lanes = pl.ds(pl.multiple_of(256 + c * 128, 128), 128)
 
@@ -452,7 +464,8 @@
     scores = fsum[...]
     for dz in range(1, NZ):
         scores = scores + frecv[dz]
-    out_ref[...] = scores
+    for f in range(NF):
+        out_ref[:, SUB * f : SUB * f + SUB] = scores[2 * f : 2 * f + 2, 0:SUB]
 
     for k in range(1, NF):
         q_copy(k).wait_send()
@@ -474,10 +487,10 @@
         sib_copy().wait_send()
 
     for dz in range(1, NZ):
-        zs_copy(dz).wait_send()
         fz_copy(dz).wait_send()
-    ring_close(zq, rq_s, rq_r)
-    ring_close(za, ra_s, ra_r)
+    zs_copy.wait_send()
+    gather_close(zq, rq_s, rq_r)
+    gather_close(za, ra_s, ra_r)
     for s in range(8):
         pa_copy(s).wait_send()
     for copy in ga_copies:
@@ -500,44 +513,44 @@
     vm = pltpu.VMEM
     out = pl.pallas_call(
         kernel,
-        out_shape=jax.ShapeDtypeStruct((16, 128), F32),
+        out_shape=jax.ShapeDtypeStruct((2, ROWS), F32),
         in_specs=[pl.BlockSpec(memory_space=pl.ANY)] * 7,
         out_specs=pl.BlockSpec(memory_space=pltpu.VMEM),
         scratch_shapes=[
-            vm((ROWS, FI), BF16), vm((ROWS, FO), BF16), vm((128, FI), BF16),
-            vm((128, FO), BF16), vm((FI, EI), BF16), vm((FO, EO), BF16),
+            vm((FI, ROWS), BF16), vm((FO, ROWS), BF16), vm((128, FI), BF16),
+            vm((128, FO), BF16), vm((EI, FI), BF16), vm((EO, FO), BF16),
             vm((EO, 640), F32),
             vm((QP, 128), F32), vm((NF, QROWS, 128), F32), vm((2, QP, 128), BF16),
-            vm((ROWS, EI), BF16), vm((NF, SUB, EI), BF16), vm((EI, 128), BF16),
-            vm((NF, SUB, EO), BF16), vm((NF, SUB, EO), BF16), vm((SUB, EO), F32),
+            vm((NF, EI, 128), BF16), vm((NF, EI, 128), BF16), vm((EI, 128), BF16),
+            vm((NF, EO, 128), BF16), vm((NF, EO, 128), BF16),
             vm((EO, 128), BF16), vm((EO, 512), BF16),
             vm((EO, 640), BF16), vm((2, EO, 640), BF16), vm((EO, HALF), F32),
             vm((HALF, 512), BF16), vm((HALF, 256), BF16), vm((8, EO, HALF), BF16),
             vm((8, 128), F32), vm((NT, 8, 128), F32),
-            vm((8, 128), F32), vm((NZ, 8, 128), F32),
+            vm((8, 128), F32), vm((8, 128), F32),
             vm((4, 4, 8, 128), F32), vm((2, NF, 8, 128), F32),
             vm((16, 128), F32), vm((NZ, 16, 128), F32),
             dma((7,)),
             dma((NF,)), dma((NF,)), dma((2, NF)), dma((2, NF)),
             dma((NF,)), dma((NF,)), dma((NF,)), dma((NF,)),
             dma((1,)), dma((1,)), dma((3,)), dma((3,)),
-            dma((2,)), dma((2,)), dma((NT,)), dma((NT,)), dma((NZ,)), dma((NZ,)),
-            dma((2, 8)), dma((8,)), dma((2, 8)), dma((8,)),
+            dma((2,)), dma((2,)), dma((NT,)), dma((NT,)), dma((1,)), dma((1,)),
+            dma((4, 8)), dma((8,)), dma((4, 8)), dma((8,)),
             dma((8,)), dma((8,)), dma((4, 4)), dma((2, NF)), dma((NZ,)), dma((NZ,)),
         ],
         compiler_params=pltpu.CompilerParams(
             collective_id=0, has_side_effects=True, vmem_limit_bytes=56 * 1024 * 1024
         ),
     )(
-        train_acts,
-        train_grads,
+        train_acts.T,
+        train_grads.T,
         query_acts.reshape(16 * LQ, FI),
         query_grads.reshape(16 * LQ, FO),
-        in_basis,
-        out_basis,
+        in_basis.T,
+        out_basis.T,
         eigenvalues,
     )
-    return out.reshape(NF, 2, 128)[:, :, :SUB].transpose(0, 2, 1).reshape(ROWS, 2)
+    return out.T
 
 
 def solution(mesh):

time: 120 us -> 86.1 us (0.72)
  Pallas kernels: 112 us -> 84.5 us
  local copies, waits for them, and re-layouts: 8.38 us -> 1.29 us
    pallas_call x1, Pallas kernels: 112 us -> 84.5 us  [shards(): pl.pallas_call(kernel, out_shape=jax.ShapeDtypeStruct((2, ROWS), F32), in...]
    unnamed x8 -> x1, local copies, waits for them, and re-layouts: 7 us -> 1.29 us
where the time goes in v2:
time: 86.1 us; the launch traced here: 85.8 us
  Pallas kernels  84.5 us (98%)
  local copies, waits for them, and re-layouts  1.29 us (1%)
    pallas_call x1, Pallas kernels, shards(): pl.pallas_call(kernel, out_shape=jax.ShapeDtypeStruct((2, ROWS), F32), in...  84.5 us

profile of v2, /device:TPU:1, one launch (start us, length us, event | category | flops | bytes accessed | tf_op | source)
XLA Modules:
  0.0 85.8 jit_solution(14198016058078719104)
XLA Ops:
  0.0 84.5 %shard_map.73 = f32[2,768]{1,0:T(2,128)} custom-call(bf16[320,768]{1,0:T(8,128)(2,1)} %bitcast.10, bf16[864,768]{1,0:T(8,128)(2,1)} %bitcast.7, bf16[512,320]{1,0:T(8,128)(2,1)} %bitcast.11, bf16[512,864]{1,0:T(8,128)(2,1)} %bitcast.8, bf16[160,320]{1,0:T(8,128)(2,1)} %bitcast.12, bf16[432,864]{1,0:T(8,128)(2,1)} %bitcast.9, f32[432,640]{1,0:T(8,128)} %ev_h.1), custom_call_target="tpu_custom_call" | custom-call | tf_op jit(solution)/shard_map/pallas_call | solution.py:514
  84.6 1.3 %copy.9 = f32[768,2]{0,1:T(2,128)} copy(f32[768,2]{0,1:T(2,128)} %bitcast.13) | data formatting | bytes 12288
